TPU v7x, 32 devices: a whole 2x2x4 slice. The times are simulated.
32 devices in a mesh: task: 4 (over y, core), rows: 8 (over z, x).
Axes of the slice: x: 2, y: 2, z: 4, core: 2. Of those that a mesh axis runs over, the one named last changes fastest.
Arguments:
- probes: bfloat16 [4, 384, 8192], P('task', None, 'rows'), may hold values from -48 to 48
- task_weights: bfloat16 [4, 8192, 128], P('task', 'rows'), may hold values from -6 to 6
Outputs:
- merged: float32 [8192, 128], P(('rows', 'task'))
- residual: float32 [8192, 128], P(('rows', 'task'))
All inputs are finite; a program needn't handle non-finite values.
Results may differ from a plain program's by a relative error of at most 0.0003.
Values may be sent and summed in bfloat16 or wider, within the bound.
A program may use at most 128 MiB of HBM per device.

v0:
```python
import jax
import jax.numpy as jnp
from jax import lax
from jax.sharding import PartitionSpec as P

PROBE = 384
ITERS = 2


ALPHA = 0.9
EPS = 1e-06


def column_squares(vector):
    return lax.psum(jnp.sum(vector * vector, axis=0), ("task", "rows"))


def on_device(probes, task_weights):
    local_x = probes[0]
    local_w = task_weights[0]
    tasks = lax.axis_size("task")
    width = local_x.shape[1]
    share = width // tasks
    cols = local_w.shape[1]
    scale = 1.0 / (PROBE * tasks)
    exact_x = local_x.astype(jnp.float32)
    diag_local = jnp.sum(exact_x * exact_x, axis=0)
    partial_value = jnp.dot(local_x, local_w, preferred_element_type=jnp.float32)
    outputs = lax.psum(partial_value, "rows")
    b_term = ALPHA * jnp.einsum("pd,pc->dc", exact_x, outputs, precision=lax.Precision.HIGHEST)
    b_term = scale * (b_term + (1.0 - ALPHA) * diag_local[:, None] * local_w.astype(jnp.float32))
    targets, diag_sum = (
        lax.psum_scatter(b_term, "task", scatter_dimension=0, tiled=True),
        lax.psum_scatter(
            (1.0 - ALPHA) * scale * diag_local, "task", scatter_dimension=0, tiled=True
        ),
    )
    merged = jnp.zeros((share, cols), jnp.float32)
    residual = targets
    direction = targets
    norm_now = column_squares(residual)
    for step in range(ITERS):
        block = lax.all_gather(direction, "task", axis=0, tiled=True)
        projected = jnp.dot(
            exact_x, block, precision=lax.Precision.HIGHEST, preferred_element_type=jnp.float32
        )
        projected = lax.psum(projected, "rows")
        summed = lax.psum_scatter(
            ALPHA
            * scale
            * jnp.einsum("pd,pc->dc", exact_x, projected, precision=lax.Precision.HIGHEST),
            "task",
            scatter_dimension=0,
            tiled=True,
        )
        image = summed + diag_sum[:, None] * direction
        curve = lax.psum(jnp.sum(direction * image, axis=0), ("task", "rows"))
        alpha = norm_now / curve
        merged = merged + alpha * direction
        residual = residual - alpha * image
        norm_next = column_squares(residual)
        direction = residual + norm_next / (norm_now + EPS) * direction
        norm_now = norm_next
    return (merged, residual)


def solution(mesh):
    in_specs = (P("task", None, "rows"), P("task", "rows", None))
    out_specs = (P(("rows", "task"), None), P(("rows", "task"), None))
    return jax.shard_map(
        on_device, mesh=mesh, in_specs=in_specs, out_specs=out_specs, check_vma=False
    )
```

profile of v0, /device:TPU:0, one launch (start us, length us, event | category | flops | bytes accessed | tf_op | source)
XLA Modules:
  0.0 445.0 jit_solution(7962792912075443583)
XLA Ops:
  7.2 2.3 fusion.10
  9.5 0.0 reduce-scatter.4.cloned.1.call-start
  9.6 0.2 multiply_reduce_fusion
  9.8 0.7 copy-done.3
  10.5 0.1 copy.7
  10.6 73.5 %all-reduce.6.cloned.1.call-done = f32[384,128]{1,0:T(8,128)} async-done(((f32[384,128]{1,0:T(8,128)}), f32[384,128]{1,0:T(8,128)}) %all-reduce.6.cloned.1.call-update) | async-done | bytes 196624 | tf_op jit(solution)/shard_map/psum | solution.py:29
  84.1 2.4 fusion.4
  86.5 0.0 all-reduce.8.cloned.1.call-start
  86.5 21.0 %reduce-scatter.4.cloned.1.call-done = f32[256,128]{0,1:T(8,128)} async-done(((f32[1024,128]{0,1:T(8,128)}), f32[256,128]{0,1:T(8,128)}) %reduce-scatter.4.cloned.1.call-update) | async-done | bytes 131088 | tf_op jit(solution)/shard_map/reduce_scatter | solution.py:33
  107.5 7.0 %all_gather.6 = f32[1024,128]{0,1:T(8,128)S(1)} all-gather(f32[256,128]{0,1:T(8,128)} %reduce-scatter.4.cloned.1.call-done), channel_id=1, replica_groups=mesh['task'=4,'rows'=8] {'task'}, dimensions={0}, use_global_device_ids=true | all-gather | bytes 655360 | tf_op jit(solution)/shard_map/all_gather | solution.py:43
  114.5 1.5 convolution_bitcast_fusion.1
  116.1 70.5 %all-reduce.8.cloned.1.call-done = f32[384,128]{0,1:T(8,128)} async-done(((f32[384,128]{0,1:T(8,128)}), f32[384,128]{0,1:T(8,128)}) %all-reduce.8.cloned.1.call-update) | async-done | bytes 196624 | tf_op jit(solution)/shard_map/psum | solution.py:47
  186.6 2.3 fusion.1
  189.0 0.6 dynamic-slice
  190.2 5.7 %all-reduce = f32[1024]{0:T(1024)S(1)} all-reduce(f32[1024]{0:T(1024)S(1)} %get-tuple-element.12), channel_id=4, replica_groups=mesh['task'=4,'rows'=8] {'task'}, use_global_device_ids=true, to_apply=%region_7.0.clone | all-reduce | flops 1024 | bytes 8192
  195.9 0.1 dynamic-slice.1
  195.9 13.9 %reduce-scatter.6.cloned.1.call-done = f32[256,128]{0,1:T(8,128)} async-done(((f32[1024,128]{0,1:T(8,128)}), f32[256,128]{0,1:T(8,128)}) %reduce-scatter.6.cloned.1.call-update) | async-done | bytes 131088 | tf_op jit(solution)/shard_map/reduce_scatter | solution.py:48
  209.9 1.0 multiply_reduce_fusion.3
  210.9 39.4 %all-reduce.1 = (f32[128]{0:T(128)S(1)}, f32[128]{0:T(128)S(1)}) all-reduce(f32[128]{0:T(128)S(1)} %get-tuple-element.7, f32[128]{0:T(128)S(1)} %get-tuple-element.6), channel_id=1, replica_groups=mesh['task'=4,'rows'=8] {'task','rows'}, use_global_device_ids=true, to_apply=%region_4.0 | all-reduce | flops 256 | bytes 2048 | tf_op jit(solution)/shard_map/psum | solution.py:15
  250.2 1.1 multiply_reduce_fusion.2
  251.3 41.0 %psum.53 = f32[128]{0:T(128)S(1)} all-reduce(f32[128]{0:T(128)S(1)} %multiply_reduce_fusion.2), channel_id=1, replica_groups=mesh['task'=4,'rows'=8] {'task','rows'}, use_global_device_ids=true, to_apply=%region_11.0 | all-reduce | flops 128 | bytes 1024 | tf_op jit(solution)/shard_map/psum | solution.py:15
  292.3 1.0 multiply_add_fusion.2
  293.3 8.0 %all_gather.7 = f32[1024,128]{0,1:T(8,128)S(1)} all-gather(f32[256,128]{0,1:T(8,128)S(1)} %multiply_add_fusion.2), channel_id=1, replica_groups=mesh['task'=4,'rows'=8] {'task'}, dimensions={0}, use_global_device_ids=true | all-gather | bytes 655360 | tf_op jit(solution)/shard_map/all_gather | solution.py:43
  301.3 1.5 convolution_bitcast_fusion
  302.9 69.1 %all-reduce.10.cloned.1.call-done = f32[384,128]{0,1:T(8,128)} async-done(((f32[384,128]{0,1:T(8,128)}), f32[384,128]{0,1:T(8,128)}) %all-reduce.10.cloned.1.call-update) | async-done | bytes 196624 | tf_op jit(solution)/shard_map/psum | solution.py:47
  372.0 2.3 fusion
  374.3 21.0 %reduce-scatter.8.cloned.1.call-done = f32[256,128]{0,1:T(8,128)} async-done(((f32[1024,128]{0,1:T(8,128)}), f32[256,128]{0,1:T(8,128)}) %reduce-scatter.8.cloned.1.call-update) | async-done | bytes 131088 | tf_op jit(solution)/shard_map/reduce_scatter | solution.py:48
  395.3 1.0 multiply_reduce_fusion.1
  396.3 39.4 %psum.55 = f32[128]{0:T(128)S(1)} all-reduce(f32[128]{0:T(128)S(1)} %multiply_reduce_fusion.1), channel_id=1, replica_groups=mesh['task'=4,'rows'=8] {'task','rows'}, use_global_device_ids=true, to_apply=%region_15.0 | all-reduce | flops 128 | bytes 1024 | tf_op jit(solution)/shard_map/psum | solution.py:57
  435.6 1.0 multiply_subtract_fusion
  436.7 0.8 copy.9
  437.4 0.8 copy.8
  (23 shorter events, 0.3 us)
Async XLA Ops:
  7.2 2.4 copy-start
  7.2 76.9 %all-reduce.6.cloned.1.call-start = ((), (), s32[]{:S(2)}) async-start(), calls=%async_computation.3 | async-start | bytes 393216 | tf_op jit(solution)/shard_map/psum | solution.py:29
  9.5 0.9 copy-start.3
  9.5 98.0 %reduce-scatter.4.cloned.1.call-start = ((), (), s32[]{:S(2)}) async-start(), calls=%async_computation.4 | async-start | bytes 655360 | tf_op jit(solution)/shard_map/reduce_scatter | solution.py:33
  86.5 100.1 %all-reduce.8.cloned.1.call-start = ((), (), s32[]{:S(2)}) async-start(), calls=%async_computation.5 | async-start | bytes 393216 | tf_op jit(solution)/shard_map/psum | solution.py:47
  116.0 73.0 %copy-start.4 = (u32[32]{0:T(128)S(1)}, u32[32]{0:T(128)}, u32[]{:S(2)}) copy-start(u32[32]{0:T(128)} %constant.18) | copy-start | bytes 388
  116.0 93.9 %copy-start.1 = (f32[256,128]{0,1:T(8,128)S(1)}, f32[256,128]{0,1:T(8,128)}, u32[]{:S(2)}) copy-start(f32[256,128]{0,1:T(8,128)} %reduce-scatter.4.cloned.1.call-done) | copy-start | bytes 393220
  116.0 93.8 %reduce-scatter.6.cloned.1.call-start = ((), (), s32[]{:S(2)}) async-start(), calls=%async_computation.6 | async-start | bytes 655360 | tf_op jit(solution)/shard_map/reduce_scatter | solution.py:48
  188.9 183.1 %all-reduce.10.cloned.1.call-start = ((), (), s32[]{:S(2)}) async-start(), calls=%async_computation.7 | async-start | bytes 393216 | tf_op jit(solution)/shard_map/psum | solution.py:47
  302.8 132.8 %copy-start.2 = (f32[256,128]{0,1:T(8,128)S(1)}, f32[256,128]{0,1:T(8,128)}, u32[]{:S(2)}) copy-start(f32[256,128]{0,1:T(8,128)} %reduce-scatter.6.cloned.1.call-done) | copy-start | bytes 393220
  302.8 92.5 %reduce-scatter.8.cloned.1.call-start = ((), (), s32[]{:S(2)}) async-start(), calls=%async_computation.8 | async-start | bytes 655360 | tf_op jit(solution)/shard_map/reduce_scatter | solution.py:48
Sparse Core Ops, SparseCore 0:
  11.3 72.7 all-reduce.5
  86.7 20.7 reduce-scatter.3
  116.1 70.4 all-reduce.7
  189.1 20.7 reduce-scatter.5
  302.9 69.0 all-reduce.9
  374.5 20.7 reduce-scatter.7
where the time goes:
time: 446 us; the launch traced here: 445 us
  waiting for transfers between devices  269 us (60%)
  blocking collectives  140 us (31%)
  between operations  14.9 us (3%)
  matrix products  12.2 us (3%)
  other arithmetic  5.34 us (1%)
    psum x2, waiting for transfers between devices, on_device(): projected = lax.psum(projected, 'rows')  140 us
    psum x2, blocking collectives, column_squares(): return lax.psum(jnp.sum(vector * vector, axis=0), ('task', 'rows'))  80.4 us
    psum x1, waiting for transfers between devices, on_device(): outputs = lax.psum(partial_value, 'rows')  73.5 us
    psum x1, blocking collectives, on_device(): curve = lax.psum(jnp.sum(direction * image, axis=0), ('task', 'rows'))  39.4 us
    reduce_scatter x2, waiting for transfers between devices, on_device(): lax.psum_scatter(ALPHA * scale * jnp.einsum('pd,pc->dc', exact_x, project...  34.9 us
    reduce_scatter x1, waiting for transfers between devices, on_device(): lax.psum_scatter(b_term, 'task', scatter_dimension=0, tiled=True)  21 us
    all_gather x2, blocking collectives, on_device(): block = lax.all_gather(direction, 'task', axis=0, tiled=True)  14.9 us
  transfers between devices with their start and end apart: 6, of which 6 were waited for; matrix products, arithmetic and copies ran while one was open for 0% of the time, Pallas kernels for 0%

commit v1 on v0

v1 whole, which is shorter than its diff:
```python
import functools

import jax
import jax.numpy as jnp
from jax import lax
from jax.experimental import pallas as pl
from jax.experimental.pallas import tpu as pltpu
from jax.sharding import PartitionSpec as P

ALPHA = 0.9
EPS = 1e-06
LANES = 128
SUB = 8
CHUNKS = 4
F32 = jnp.float32
BF16 = jnp.bfloat16
MESH = pl.DeviceIdType.MESH


def two_terms(value):
    high = value.astype(BF16).astype(F32)
    return jnp.concatenate([high, value - high], axis=0).astype(BF16)


def fold(product):
    half = product.shape[0] // 2
    return product[:half] + product[half:]


def times_probes(value, xs):
    return fold(jnp.dot(two_terms(value), xs[...], preferred_element_type=F32))


def times_features(value, xs):
    return fold(
        lax.dot_general(
            two_terms(value), xs[...], (((1,), (1,)), ((), ())), preferred_element_type=F32
        )
    )


def remote(src, dst, send, recv, device):
    return pltpu.make_async_remote_copy(
        src_ref=src, dst_ref=dst, send_sem=send, recv_sem=recv, device_id=device, device_id_type=MESH
    )


def kernel(
    tasks, rows,
    x_hbm, w_hbm, merged_ref, residual_ref,
    xs, w_own, wt_send, wt_all, y_send, y_recv, y_red, y_all,
    z_send, z_recv, z_red, z_full, z_flat, fin_send, fin_recv,
    local_sem, cross_send, cross_recv, core_send, core_recv, w_send_sem, w_recv_sem,
    yr_send, yr_recv, ya_send, ya_recv, zr_send, zr_recv, za_send, za_recv, f_send, f_recv,
):
    t, r = lax.axis_index("task"), lax.axis_index("rows")
    probe, width = x_hbm.shape[1:]
    cols = w_hbm.shape[2]
    group = cols // tasks
    piece = cols // rows
    per = group // piece
    parts = rows // (group // SUB)
    span = tasks * probe // parts
    share = width // tasks
    pairs = tasks // 2
    chunk = probe // CHUNKS
    c1 = ALPHA / (probe * tasks)
    c2 = (1.0 - ALPHA) / (probe * tasks)
    total = tasks * rows

    barrier = pltpu.get_barrier_semaphore()
    me = t * rows + r

    @pl.loop(1, total)
    def _(i):
        other = lax.rem(me + i, total)
        pl.semaphore_signal(
            barrier, inc=1, device_id=(other // rows, lax.rem(other, rows)), device_id_type=MESH
        )

    load_x = pltpu.make_async_copy(
        x_hbm.at[0], xs.at[pl.ds(pl.multiple_of(t * probe, probe), probe)], local_sem.at[0]
    )
    load_x.start()
    load_w = pltpu.make_async_copy(w_hbm.at[0], w_own, local_sem.at[1])
    load_w.start()
    pl.semaphore_wait(barrier, total - 1)

    pair, core = t // 2, lax.rem(t, 2)
    mate = (pair * 2 + 1 - core, r)

    def rows_of(task, c):
        return pl.ds(pl.multiple_of(task * probe + c * chunk, chunk), chunk)

    def cross(j, c):
        to = (lax.rem(pair + j, pairs) * 2 + core, r)
        return remote(
            x_hbm.at[0, pl.ds(c * chunk, chunk)], xs.at[rows_of(t, c)],
            cross_send.at[j, c], cross_recv.at[j, c], to,
        )

    def crossed(j, c):
        return xs.at[rows_of(lax.rem(pair - j + pairs, pairs) * 2 + core, c)]

    def arrived(j, c):
        place = crossed(j, c)
        return remote(place, place, cross_send.at[j, c], cross_recv.at[j, c], mate)

    def own_to_mate(c):
        return remote(
            x_hbm.at[0, pl.ds(c * chunk, chunk)], xs.at[rows_of(t, c)],
            core_send.at[0, c], core_recv.at[0, c], mate,
        )

    def relay(j, c):
        place = crossed(j, c)
        return remote(place, place, core_send.at[j, c], core_recv.at[j, c], mate)

    def from_mate(j, c):
        source = lax.rem(pair - j + pairs, pairs) * 2 + 1 - core
        place = xs.at[rows_of(source, c)]
        return remote(place, place, core_send.at[j, c], core_recv.at[j, c], mate)

    for c in range(CHUNKS):
        for j in range(1, pairs):
            cross(j, c).start()
    for c in range(CHUNKS):
        own_to_mate(c).start()

    load_w.wait()
    load_x.wait()
    own = xs[pl.ds(pl.multiple_of(t * probe, probe), probe), :]
    outputs = jnp.dot(own, w_own[...], preferred_element_type=F32)
    y_send[...] = outputs.T.reshape(y_send.shape)

    def y_scatter(k):
        to = lax.rem(r + k, rows)
        return remote(y_send.at[to], y_recv.at[k], yr_send.at[k], yr_recv.at[k], (t, to))

    for k in range(1, rows):
        y_scatter(k).start()

    wt_send[...] = w_own[...].astype(F32).T.reshape(wt_send.shape).astype(wt_send.dtype)

    def w_scatter(j):
        to = lax.rem(t + j, tasks)
        return remote(wt_send.at[to], wt_all.at[t], w_send_sem.at[j], w_recv_sem.at[j], (to, r))

    for j in range(1, tasks):
        w_scatter(j).start()
    wt_all[t] = wt_send[t]

    total_y = y_send[r]
    for k in range(1, rows):
        y_scatter(k).wait_recv()
        total_y = total_y + y_recv[k]
    y_red[...] = total_y
    owner = r // per
    place_y = y_all.at[
        pl.ds(pl.multiple_of(lax.rem(r, per) * piece, piece), piece),
        pl.ds(pl.multiple_of(t * probe, LANES), probe),
    ]

    def y_gather(k):
        return remote(
            y_red, place_y, ya_send.at[k], ya_recv.at[t * per + lax.rem(r, per)],
            (owner, lax.rem(r + k, rows)),
        )

    for k in range(1, rows):
        y_gather(k).start()

    @pl.when(owner != t)
    def _():
        y_gather(0).start()

    @pl.when(owner == t)
    def _():
        y_all[
            pl.ds(pl.multiple_of(lax.rem(r, per) * piece, piece), piece),
            pl.ds(pl.multiple_of(t * probe, LANES), probe),
        ] = total_y

    for c in range(CHUNKS):
        for j in range(1, pairs):
            arrived(j, c).wait_recv()
            relay(j, c).start()
    for c in range(CHUNKS):
        for j in range(pairs):
            from_mate(j, c).wait_recv()
    for j in range(1, tasks):
        source = lax.rem(t - j + tasks, tasks)
        remote(
            wt_send.at[0], wt_all.at[source], w_send_sem.at[j], w_recv_sem.at[j], (t, r)
        ).wait_recv()

    diag = jnp.zeros((1, width), F32)
    term = jnp.zeros((group, width), F32)
    for task in range(tasks):

        def squares(i, acc):
            block = xs[pl.ds(pl.multiple_of(task * probe + i * 16, 16), 16), :].astype(F32)
            return acc + block * block

        own_diag = jnp.sum(
            lax.fori_loop(0, probe // 16, squares, jnp.zeros((16, width), F32)), axis=0, keepdims=True
        )
        diag = diag + own_diag
        term = term + own_diag * wt_all[task].astype(F32)
    diag = c2 * diag

    for task in range(tasks):
        for k in range(per):

            @pl.when(jnp.logical_or(task != t, t * per + k != r))
            def _():
                place = y_all.at[pl.ds(k * piece, piece), pl.ds(task * probe, probe)]
                remote(
                    y_red, place, ya_send.at[0], ya_recv.at[task * per + k], (t, r)
                ).wait_recv()

    targets = c1 * times_probes(y_all[...], xs) + c2 * term

    lane = lax.broadcasted_iota(jnp.int32, (group, LANES), 1)

    def reduce_rows(n, product, sums):
        extra = jnp.zeros((group, LANES), F32)
        for i, value in enumerate(sums):
            extra = jnp.where(lane == i, value, extra)
        for q in range(rows):
            top, left = SUB * (q // parts), span * (q % parts)
            z_send[n, q, :, :span] = product[top : top + SUB, left : left + span]
            z_send[n, q, :, span:] = extra[top : top + SUB]

        def scatter(k):
            to = lax.rem(r + k, rows)
            return remote(
                z_send.at[n, to], z_recv.at[n, k], zr_send.at[n, k], zr_recv.at[n, k], (t, to)
            )

        for k in range(1, rows):
            scatter(k).start()
        acc = z_send[n, r]
        for k in range(1, rows):
            scatter(k).wait_recv()
            acc = acc + z_recv[n, k]
        z_red[n] = acc

        def gather(k):
            return remote(
                z_red.at[n], z_full.at[n, r], za_send.at[n, k], za_recv.at[n, k],
                (t, lax.rem(r + k, rows)),
            )

        for k in range(1, rows):
            gather(k).start()
        z_full[n, r] = acc
        for k in range(1, rows):
            source = lax.rem(r - k + rows, rows)
            remote(
                z_red.at[n], z_full.at[n, source], za_send.at[n, k], za_recv.at[n, k], (t, r)
            ).wait_recv()
        for q in range(rows):
            top, left = SUB * (q // parts), span * (q % parts)
            z_flat[n, top : top + SUB, left : left + span] = z_full[n, q, :, :span]
        found = jnp.concatenate(
            [z_full[n, q, :, span:] for q in range(0, rows, parts)], axis=0
        )
        for k in range(1, rows):
            scatter(k).wait_send()
            gather(k).wait_send()
        return z_flat[n], [found[:, i : i + 1] for i in range(len(sums))]

    def column_sum(value):
        return jnp.sum(value, axis=1, keepdims=True)

    product, (norm_0, weighted_00) = reduce_rows(
        0,
        times_features(targets, xs),
        [column_sum(targets * targets), column_sum(diag * targets * targets)],
    )
    step_1 = norm_0 / (c1 * column_sum(product * product) + weighted_00)
    residual = targets - step_1 * (c1 * times_probes(product, xs) + diag * targets)

    weighted = diag * residual
    product_r, (norm_1, weighted_11, weighted_01) = reduce_rows(
        1,
        times_features(residual, xs),
        [column_sum(residual * residual), column_sum(weighted * residual), column_sum(weighted * targets)],
    )
    beta = norm_1 / (norm_0 + EPS)
    product = product_r + beta * product
    direction = residual + beta * targets
    curve = c1 * column_sum(product * product) + (
        weighted_11 + beta * (2.0 * weighted_01 + beta * weighted_00)
    )
    step_2 = norm_1 / curve

    def finish(n, value):
        for q in range(tasks):
            fin_send[n, q, :, :share] = value[:, q * share : (q + 1) * share]
        for j in range(1, tasks):
            to = lax.rem(t + j, tasks)
            remote(
                fin_send.at[n, to], fin_recv.at[n, t], f_send.at[n, j], f_recv.at[n, j], (to, r)
            ).start()
        fin_recv[n, t] = fin_send[n, t]

    def collect(n, out_ref):
        for j in range(1, tasks):
            source = lax.rem(t - j + tasks, tasks)
            remote(
                fin_send.at[n, source], fin_recv.at[n, source], f_send.at[n, j], f_recv.at[n, j], (t, r)
            ).wait()
        whole = fin_recv[n].reshape(cols, fin_recv.shape[3]).T
        out_ref[...] = whole[:share]

    finish(0, step_1 * targets + step_2 * direction)
    finish(1, residual - step_2 * (c1 * times_probes(product, xs) + diag * direction))
    for c in range(CHUNKS):
        own_to_mate(c).wait_send()
        for j in range(1, pairs):
            cross(j, c).wait_send()
            relay(j, c).wait_send()
    for k in range(1, rows):
        y_scatter(k).wait_send()
        y_gather(k).wait_send()

    @pl.when(owner != t)
    def _():
        y_gather(0).wait_send()

    for j in range(1, tasks):
        w_scatter(j).wait_send()
    collect(0, merged_ref)
    collect(1, residual_ref)


def on_device(tasks, rows, probes, task_weights):
    probe, width = probes.shape[1:]
    cols = task_weights.shape[2]
    group = cols // tasks
    piece = cols // rows
    per = group // piece
    parts = rows // (group // SUB)
    span = tasks * probe // parts
    share = width // tasks
    pairs = tasks // 2
    padded = max(share, LANES)
    w_type = BF16 if group % 16 == 0 else F32
    vmem, dma = pltpu.VMEM, pltpu.SemaphoreType.DMA
    merged, residual = pl.pallas_call(
        functools.partial(kernel, tasks, rows),
        out_shape=[jax.ShapeDtypeStruct((share, cols), F32)] * 2,
        in_specs=[pl.BlockSpec(memory_space=pl.ANY)] * 2,
        out_specs=[pl.BlockSpec(memory_space=pltpu.VMEM)] * 2,
        scratch_shapes=[
            vmem((tasks * probe, width), BF16),
            vmem((width, cols), BF16),
            vmem((tasks, group, width), w_type),
            vmem((tasks, group, width), w_type),
            vmem((rows, piece, probe), F32),
            vmem((rows, piece, probe), F32),
            vmem((piece, probe), F32),
            vmem((group, tasks * probe), F32),
            vmem((2, rows, SUB, span + LANES), F32),
            vmem((2, rows, SUB, span + LANES), F32),
            vmem((2, SUB, span + LANES), F32),
            vmem((2, rows, SUB, span + LANES), F32),
            vmem((2, group, tasks * probe), F32),
            vmem((2, tasks, group, padded), F32),
            vmem((2, tasks, group, padded), F32),
            dma((2,)),
            dma((pairs, CHUNKS)),
            dma((pairs, CHUNKS)),
            dma((pairs, CHUNKS)),
            dma((pairs, CHUNKS)),
            dma((tasks,)),
            dma((tasks,)),
            dma((rows,)),
            dma((rows,)),
            dma((rows,)),
            dma((tasks * per,)),
            dma((2, rows)),
            dma((2, rows)),
            dma((2, rows)),
            dma((2, rows)),
            dma((2, tasks)),
            dma((2, tasks)),
        ],
        compiler_params=pltpu.CompilerParams(
            collective_id=0, has_side_effects=True, vmem_limit_bytes=48 * 2**20
        ),
    )(probes, task_weights)
    return merged, residual


def solution(mesh):
    in_specs = (P("task", None, "rows"), P("task", "rows", None))
    out_specs = (P(("rows", "task"), None), P(("rows", "task"), None))
    body = functools.partial(on_device, mesh.shape["task"], mesh.shape["rows"])
    return jax.shard_map(body, mesh=mesh, in_specs=in_specs, out_specs=out_specs, check_vma=False)
```

time: 446 us -> 68.8 us (0.15)
  waiting for transfers between devices: 269 us -> 0 us
  blocking collectives: 140 us -> 0 us
  Pallas kernels: 0 us -> 64.5 us
  between operations: 14.9 us -> 0.65 us
  matrix products: 12.2 us -> 0 us
  other arithmetic: 5.34 us -> 0 us
    psum x3 -> x0, waiting for transfers between devices: 213 us -> none  [the longest x2 140 us: on_device(): projected = lax.psum(projected, 'rows')]
    psum x3 -> x0, blocking collectives: 120 us -> none  [the longest x2 80.4 us: column_squares(): return lax.psum(jnp.sum(vector * vector, axis=0), ('task', 'rows'))]
    pallas_call x0 -> x1, Pallas kernels: none -> 64.5 us  [on_device(): pl.pallas_call(functools.partial(kernel, tasks, rows), out_shape=[jax.Sha...]
    reduce_scatter x3 -> x0, waiting for transfers between devices: 55.8 us -> none  [the longest x2 34.9 us: on_device(): lax.psum_scatter(ALPHA * scale * jnp.einsum('pd,pc->dc', exact_x, project...]
    all_gather x2 -> x0, blocking collectives: 14.9 us -> none  [on_device(): block = lax.all_gather(direction, 'task', axis=0, tiled=True)]
    dot_general x6 -> x0, matrix products: 12.2 us -> none  [the longest x2 4.59 us: on_device(): jnp.einsum('pd,pc->dc', exact_x, projected, precision=lax.Precision.HIGHEST)]
    unnamed x1 -> x0, blocking collectives: 5.67 us -> none
  transfers between devices with their start and end apart: 6 -> 0, of which waited for: 6 -> 0; matrix products, arithmetic and copies ran while one was open for 0% -> 0% of each run, Pallas kernels for 0% -> 0%
where the time goes in v1:
time: 68.8 us; the launch traced here: 68.6 us
  Pallas kernels  64.5 us (94%)
  local copies, waits for them, and re-layouts  3.39 us (5%)
    pallas_call x1, Pallas kernels, on_device(): pl.pallas_call(functools.partial(kernel, tasks, rows), out_shape=[jax.Sha...  64.5 us
    unnamed x6, local copies, waits for them, and re-layouts  3.39 us

profile of v1, /device:TPU:0, one launch (start us, length us, event | category | flops | bytes accessed | tf_op | source)
XLA Modules:
  0.0 68.6 jit_solution(444610590596200230)
XLA Ops:
  0.6 0.0 copy-start
  0.6 1.1 %copy-done = bf16[1,384,1024]{2,1,0:T(8,128)(2,1)S(1)} copy-done((bf16[1,384,1024]{2,1,0:T(8,128)(2,1)S(1)}, bf16[1,384,1024]{2,1,0:T(8,128)(2,1)}, u32[]{:S(2)}) %copy-start) | copy-done | bytes 786456
  1.8 0.0 copy-start.1
  1.8 0.9 %copy-done.1 = bf16[1,1024,128]{2,1,0:T(8,128)(2,1)S(1)} copy-done((bf16[1,1024,128]{2,1,0:T(8,128)(2,1)S(1)}, bf16[1,1024,128]{2,1,0:T(8,128)(2,1)}, u32[]{:S(2)}) %copy-start.1) | copy-done | bytes 262168
  2.7 64.5 %shard_map.41 = (f32[256,128]{1,0:T(8,128)S(1)}, f32[256,128]{1,0:T(8,128)S(1)}) custom-call(bf16[1,384,1024]{2,1,0:T(8,128)(2,1)S(1)} %copy-done, bf16[1,1024,128]{2,1,0:T(8,128)(2,1)S(1)} %copy-done.1), custom_call_target="tpu_custom_call" | custom-call | tf_op jit(solution)/shard_map/pallas_call | solution.py:352
  67.3 0.7 copy.6
  67.9 0.7 copy.7
Async XLA Ops:
  0.6 1.1 %copy-start = (bf16[1,384,1024]{2,1,0:T(8,128)(2,1)S(1)}, bf16[1,384,1024]{2,1,0:T(8,128)(2,1)}, u32[]{:S(2)}) copy-start(bf16[1,384,1024]{2,1,0:T(8,128)(2,1)} %x_hbm.1) | copy-start | bytes 2359300
  1.8 0.9 %copy-start.1 = (bf16[1,1024,128]{2,1,0:T(8,128)(2,1)S(1)}, bf16[1,1024,128]{2,1,0:T(8,128)(2,1)}, u32[]{:S(2)}) copy-start(bf16[1,1024,128]{2,1,0:T(8,128)(2,1)} %w_hbm.1) | copy-start | bytes 786436

commit v2 on v1

--- a/solution.py
+++ b/solution.py
@@ -11,7 +11,7 @@
 EPS = 1e-06
 LANES = 128
 SUB = 8
-CHUNKS = 4
+CHUNKS = 6
 F32 = jnp.float32
 BF16 = jnp.bfloat16
 MESH = pl.DeviceIdType.MESH
@@ -29,14 +29,6 @@
 
 def times_probes(value, xs):
     return fold(jnp.dot(two_terms(value), xs[...], preferred_element_type=F32))
-
-
-def times_features(value, xs):
-    return fold(
-        lax.dot_general(
-            two_terms(value), xs[...], (((1,), (1,)), ((), ())), preferred_element_type=F32
-        )
-    )
 
 
 def remote(src, dst, send, recv, device):
@@ -49,7 +41,7 @@
     tasks, rows,
     x_hbm, w_hbm, merged_ref, residual_ref,
     xs, w_own, wt_send, wt_all, y_send, y_recv, y_red, y_all,
-    z_send, z_recv, z_red, z_full, z_flat, fin_send, fin_recv,
+    squares, z_send, z_recv, z_red, z_flat, fin_send, fin_recv,
     local_sem, cross_send, cross_recv, core_send, core_recv, w_send_sem, w_recv_sem,
     yr_send, yr_recv, ya_send, ya_recv, zr_send, zr_recv, za_send, za_recv, f_send, f_recv,
 ):
@@ -66,16 +58,19 @@
     chunk = probe // CHUNKS
     c1 = ALPHA / (probe * tasks)
     c2 = (1.0 - ALPHA) / (probe * tasks)
-    total = tasks * rows
 
     barrier = pltpu.get_barrier_semaphore()
-    me = t * rows + r
-
-    @pl.loop(1, total)
+
+    @pl.loop(1, tasks)
     def _(i):
-        other = lax.rem(me + i, total)
         pl.semaphore_signal(
-            barrier, inc=1, device_id=(other // rows, lax.rem(other, rows)), device_id_type=MESH
+            barrier, inc=1, device_id=(lax.rem(t + i, tasks), r), device_id_type=MESH
+        )
+
+    @pl.loop(1, rows)
+    def _(i):
+        pl.semaphore_signal(
+            barrier, inc=1, device_id=(t, lax.rem(r + i, rows)), device_id_type=MESH
         )
 
     load_x = pltpu.make_async_copy(
@@ -84,7 +79,23 @@
     load_x.start()
     load_w = pltpu.make_async_copy(w_hbm.at[0], w_own, local_sem.at[1])
     load_w.start()
-    pl.semaphore_wait(barrier, total - 1)
+
+    def row_squares(first, count):
+        def add(i, acc):
+            block = xs[pl.ds(pl.multiple_of(first + i * 16, 16), 16), :].astype(F32)
+            return acc + block * block
+
+        return lax.fori_loop(0, count // 16, add, jnp.zeros((16, width), F32))
+
+    load_w.wait()
+    wt_send[...] = w_own[...].astype(F32).T.reshape(wt_send.shape).astype(wt_send.dtype)
+    wt_all[t] = wt_send[t]
+    load_x.wait()
+    own = xs[pl.ds(pl.multiple_of(t * probe, probe), probe), :]
+    outputs = jnp.dot(own, w_own[...], preferred_element_type=F32)
+    y_send[...] = outputs.T.reshape(y_send.shape)
+    squares[t] = row_squares(t * probe, probe)
+    pl.semaphore_wait(barrier, tasks + rows - 2)
 
     pair, core = t // 2, lax.rem(t, 2)
     mate = (pair * 2 + 1 - core, r)
@@ -121,34 +132,26 @@
         place = xs.at[rows_of(source, c)]
         return remote(place, place, core_send.at[j, c], core_recv.at[j, c], mate)
 
-    for c in range(CHUNKS):
-        for j in range(1, pairs):
-            cross(j, c).start()
-    for c in range(CHUNKS):
-        own_to_mate(c).start()
-
-    load_w.wait()
-    load_x.wait()
-    own = xs[pl.ds(pl.multiple_of(t * probe, probe), probe), :]
-    outputs = jnp.dot(own, w_own[...], preferred_element_type=F32)
-    y_send[...] = outputs.T.reshape(y_send.shape)
+    def w_scatter(j):
+        to = lax.rem(t + j, tasks)
+        return remote(wt_send.at[to], wt_all.at[t], w_send_sem.at[j], w_recv_sem.at[j], (to, r))
 
     def y_scatter(k):
         to = lax.rem(r + k, rows)
         return remote(y_send.at[to], y_recv.at[k], yr_send.at[k], yr_recv.at[k], (t, to))
 
+    for j in range(1, pairs):
+        cross(j, 0).start()
     for k in range(1, rows):
         y_scatter(k).start()
-
-    wt_send[...] = w_own[...].astype(F32).T.reshape(wt_send.shape).astype(wt_send.dtype)
-
-    def w_scatter(j):
-        to = lax.rem(t + j, tasks)
-        return remote(wt_send.at[to], wt_all.at[t], w_send_sem.at[j], w_recv_sem.at[j], (to, r))
-
-    for j in range(1, tasks):
-        w_scatter(j).start()
-    wt_all[t] = wt_send[t]
+    for c in range(1, CHUNKS):
+        for j in range(1, pairs):
+            cross(j, c).start()
+        if c == 1:
+            for j in range(1, tasks):
+                w_scatter(j).start()
+    for c in range(CHUNKS):
+        own_to_mate(c).start()
 
     total_y = y_send[r]
     for k in range(1, rows):
@@ -181,34 +184,24 @@
             pl.ds(pl.multiple_of(t * probe, LANES), probe),
         ] = total_y
 
+    def pass_on(j, c):
+        arrived(j, c).wait_recv()
+        relay(j, c).start()
+        source = lax.rem(pair - j + pairs, pairs) * 2 + core
+        part = row_squares(source * probe + c * chunk, chunk)
+        squares[source] = part if c == 0 else squares[source] + part
+
+    def take_in(j, c):
+        from_mate(j, c).wait_recv()
+        source = lax.rem(pair - j + pairs, pairs) * 2 + 1 - core
+        part = row_squares(source * probe + c * chunk, chunk)
+        squares[source] = part if c == 0 else squares[source] + part
+
     for c in range(CHUNKS):
+        take_in(0, c)
+    for c in range(CHUNKS // 2):
         for j in range(1, pairs):
-            arrived(j, c).wait_recv()
-            relay(j, c).start()
-    for c in range(CHUNKS):
-        for j in range(pairs):
-            from_mate(j, c).wait_recv()
-    for j in range(1, tasks):
-        source = lax.rem(t - j + tasks, tasks)
-        remote(
-            wt_send.at[0], wt_all.at[source], w_send_sem.at[j], w_recv_sem.at[j], (t, r)
-        ).wait_recv()
-
-    diag = jnp.zeros((1, width), F32)
-    term = jnp.zeros((group, width), F32)
-    for task in range(tasks):
-
-        def squares(i, acc):
-            block = xs[pl.ds(pl.multiple_of(task * probe + i * 16, 16), 16), :].astype(F32)
-            return acc + block * block
-
-        own_diag = jnp.sum(
-            lax.fori_loop(0, probe // 16, squares, jnp.zeros((16, width), F32)), axis=0, keepdims=True
-        )
-        diag = diag + own_diag
-        term = term + own_diag * wt_all[task].astype(F32)
-    diag = c2 * diag
-
+            pass_on(j, c)
     for task in range(tasks):
         for k in range(per):
 
@@ -219,64 +212,100 @@
                     y_red, place, ya_send.at[0], ya_recv.at[task * per + k], (t, r)
                 ).wait_recv()
 
+    for j in range(1, tasks):
+        source = lax.rem(t - j + tasks, tasks)
+        remote(
+            wt_send.at[0], wt_all.at[source], w_send_sem.at[j], w_recv_sem.at[j], (t, r)
+        ).wait_recv()
+    for c in range(CHUNKS // 2, CHUNKS):
+        for j in range(1, pairs):
+            pass_on(j, c)
+            take_in(j, c - CHUNKS // 2)
+    for c in range(CHUNKS - CHUNKS // 2, CHUNKS):
+        for j in range(1, pairs):
+            take_in(j, c)
+
+    diag = jnp.zeros((1, width), F32)
+    term = jnp.zeros((group, width), F32)
+    for task in range(tasks):
+        own_diag = jnp.sum(squares[task], axis=0, keepdims=True)
+        diag = diag + own_diag
+        term = term + own_diag * wt_all[task].astype(F32)
+    diag = c2 * diag
     targets = c1 * times_probes(y_all[...], xs) + c2 * term
 
     lane = lax.broadcasted_iota(jnp.int32, (group, LANES), 1)
 
-    def reduce_rows(n, product, sums):
+    def reduce_rows(n, vector, sums):
         extra = jnp.zeros((group, LANES), F32)
         for i, value in enumerate(sums):
             extra = jnp.where(lane == i, value, extra)
-        for q in range(rows):
-            top, left = SUB * (q // parts), span * (q % parts)
-            z_send[n, q, :, :span] = product[top : top + SUB, left : left + span]
-            z_send[n, q, :, span:] = extra[top : top + SUB]
-
-        def scatter(k):
-            to = lax.rem(r + k, rows)
+        extra = jnp.concatenate([extra, jnp.zeros((LANES - group, LANES), F32)], axis=0).T[:SUB]
+        terms = two_terms(vector)
+
+        def scatter(to):
+            k = lax.rem(to - r + rows, rows)
             return remote(
                 z_send.at[n, to], z_recv.at[n, k], zr_send.at[n, k], zr_recv.at[n, k], (t, to)
             )
 
-        for k in range(1, rows):
-            scatter(k).start()
+        for p in range(parts):
+            product = fold(
+                lax.dot_general(
+                    terms, xs[p * span : (p + 1) * span, :], (((1,), (1,)), ((), ())),
+                    preferred_element_type=F32,
+                )
+            )
+            for q in range(p, rows, parts):
+                top = SUB * (q // parts)
+                z_send[n, q, :, :span] = product[top : top + SUB]
+                z_send[n, q, :, span:] = extra
+
+                @pl.when(q != r)
+                def _():
+                    scatter(q).start()
+
         acc = z_send[n, r]
         for k in range(1, rows):
-            scatter(k).wait_recv()
+            remote(
+                z_send.at[n, r], z_recv.at[n, k], zr_send.at[n, k], zr_recv.at[n, k], (t, r)
+            ).wait_recv()
             acc = acc + z_recv[n, k]
-        z_red[n] = acc
+        z_red[n] = acc[:, :span]
+
+        def spot(source):
+            return (
+                n,
+                pl.ds(pl.multiple_of(SUB * (source // parts), SUB), SUB),
+                pl.ds(pl.multiple_of(span * lax.rem(source, parts), LANES), span),
+            )
 
         def gather(k):
             return remote(
-                z_red.at[n], z_full.at[n, r], za_send.at[n, k], za_recv.at[n, k],
+                z_red.at[n], z_flat.at[spot(r)], za_send.at[n, k], za_recv.at[n, k],
                 (t, lax.rem(r + k, rows)),
             )
 
         for k in range(1, rows):
             gather(k).start()
-        z_full[n, r] = acc
+        z_flat[spot(r)] = acc[:, :span]
+        found = jnp.concatenate([acc[:, span:], jnp.zeros((LANES - SUB, LANES), F32)], axis=0).T
         for k in range(1, rows):
             source = lax.rem(r - k + rows, rows)
             remote(
-                z_red.at[n], z_full.at[n, source], za_send.at[n, k], za_recv.at[n, k], (t, r)
+                z_red.at[n], z_flat.at[spot(source)], za_send.at[n, k], za_recv.at[n, k], (t, r)
             ).wait_recv()
-        for q in range(rows):
-            top, left = SUB * (q // parts), span * (q % parts)
-            z_flat[n, top : top + SUB, left : left + span] = z_full[n, q, :, :span]
-        found = jnp.concatenate(
-            [z_full[n, q, :, span:] for q in range(0, rows, parts)], axis=0
-        )
         for k in range(1, rows):
-            scatter(k).wait_send()
+            scatter(lax.rem(r + k, rows)).wait_send()
             gather(k).wait_send()
-        return z_flat[n], [found[:, i : i + 1] for i in range(len(sums))]
+        return z_flat[n], [found[:group, i : i + 1] for i in range(len(sums))]
 
     def column_sum(value):
         return jnp.sum(value, axis=1, keepdims=True)
 
     product, (norm_0, weighted_00) = reduce_rows(
         0,
-        times_features(targets, xs),
+        targets,
         [column_sum(targets * targets), column_sum(diag * targets * targets)],
     )
     step_1 = norm_0 / (c1 * column_sum(product * product) + weighted_00)
@@ -285,7 +314,7 @@
     weighted = diag * residual
     product_r, (norm_1, weighted_11, weighted_01) = reduce_rows(
         1,
-        times_features(residual, xs),
+        residual,
         [column_sum(residual * residual), column_sum(weighted * residual), column_sum(weighted * targets)],
     )
     beta = norm_1 / (norm_0 + EPS)
@@ -352,7 +381,7 @@
     merged, residual = pl.pallas_call(
         functools.partial(kernel, tasks, rows),
         out_shape=[jax.ShapeDtypeStruct((share, cols), F32)] * 2,
-        in_specs=[pl.BlockSpec(memory_space=pl.ANY)] * 2,
+        in_specs=[pl.BlockSpec(memory_space=pltpu.HBM)] * 2,
         out_specs=[pl.BlockSpec(memory_space=pltpu.VMEM)] * 2,
         scratch_shapes=[
             vmem((tasks * probe, width), BF16),
@@ -363,10 +392,10 @@
             vmem((rows, piece, probe), F32),
             vmem((piece, probe), F32),
             vmem((group, tasks * probe), F32),
+            vmem((tasks, 16, width), F32),
             vmem((2, rows, SUB, span + LANES), F32),
             vmem((2, rows, SUB, span + LANES), F32),
-            vmem((2, SUB, span + LANES), F32),
-            vmem((2, rows, SUB, span + LANES), F32),
+            vmem((2, SUB, span), F32),
             vmem((2, group, tasks * probe), F32),
             vmem((2, tasks, group, padded), F32),
             vmem((2, tasks, group, padded), F32),

time: 68.8 us -> 67.6 us (0.983)
  Pallas kernels: 64.5 us -> 63.4 us
    pallas_call x1, Pallas kernels: 64.5 us -> 63.4 us  [on_device(): pl.pallas_call(functools.partial(kernel, tasks, rows), out_shape=[jax.Sha...]
where the time goes in v2:
time: 67.6 us; the launch traced here: 67.4 us
  Pallas kernels  63.4 us (94%)
  local copies, waits for them, and re-layouts  3.39 us (5%)
    pallas_call x1, Pallas kernels, on_device(): pl.pallas_call(functools.partial(kernel, tasks, rows), out_shape=[jax.Sha...  63.4 us
    unnamed x6, local copies, waits for them, and re-layouts  3.39 us

profile of v2, /device:TPU:0, one launch (start us, length us, event | category | flops | bytes accessed | tf_op | source)
XLA Modules:
  0.0 67.4 jit_solution(5080244081261045521)
XLA Ops:
  0.6 0.0 copy-start
  0.6 1.1 %copy-done = bf16[1,384,1024]{2,1,0:T(8,128)(2,1)S(1)} copy-done((bf16[1,384,1024]{2,1,0:T(8,128)(2,1)S(1)}, bf16[1,384,1024]{2,1,0:T(8,128)(2,1)}, u32[]{:S(2)}) %copy-start) | copy-done | bytes 786456
  1.8 0.0 copy-start.1
  1.8 0.9 %copy-done.1 = bf16[1,1024,128]{2,1,0:T(8,128)(2,1)S(1)} copy-done((bf16[1,1024,128]{2,1,0:T(8,128)(2,1)S(1)}, bf16[1,1024,128]{2,1,0:T(8,128)(2,1)}, u32[]{:S(2)}) %copy-start.1) | copy-done | bytes 262168
  2.7 63.4 %shard_map.41 = (f32[256,128]{1,0:T(8,128)S(1)}, f32[256,128]{1,0:T(8,128)S(1)}) custom-call(bf16[1,384,1024]{2,1,0:T(8,128)(2,1)S(1)} %copy-done, bf16[1,1024,128]{2,1,0:T(8,128)(2,1)S(1)} %copy-done.1), custom_call_target="tpu_custom_call" | custom-call | tf_op jit(solution)/shard_map/pallas_call | solution.py:381
  66.1 0.7 copy.6
  66.8 0.7 copy.7
Async XLA Ops:
  0.6 1.1 %copy-start = (bf16[1,384,1024]{2,1,0:T(8,128)(2,1)S(1)}, bf16[1,384,1024]{2,1,0:T(8,128)(2,1)}, u32[]{:S(2)}) copy-start(bf16[1,384,1024]{2,1,0:T(8,128)(2,1)} %x_hbm.1) | copy-start | bytes 2359300
  1.8 0.9 %copy-start.1 = (bf16[1,1024,128]{2,1,0:T(8,128)(2,1)S(1)}, bf16[1,1024,128]{2,1,0:T(8,128)(2,1)}, u32[]{:S(2)}) copy-start(bf16[1,1024,128]{2,1,0:T(8,128)(2,1)} %w_hbm.1) | copy-start | bytes 786436

commit v3 on v2

--- a/solution.py
+++ b/solution.py
@@ -106,7 +106,7 @@
     def cross(j, c):
         to = (lax.rem(pair + j, pairs) * 2 + core, r)
         return remote(
-            x_hbm.at[0, pl.ds(c * chunk, chunk)], xs.at[rows_of(t, c)],
+            xs.at[rows_of(t, c)], xs.at[rows_of(t, c)],
             cross_send.at[j, c], cross_recv.at[j, c], to,
         )
 
@@ -119,7 +119,7 @@
 
     def own_to_mate(c):
         return remote(
-            x_hbm.at[0, pl.ds(c * chunk, chunk)], xs.at[rows_of(t, c)],
+            xs.at[rows_of(t, c)], xs.at[rows_of(t, c)],
             core_send.at[0, c], core_recv.at[0, c], mate,
         )
 
@@ -418,7 +418,7 @@
             dma((2, tasks)),
         ],
         compiler_params=pltpu.CompilerParams(
-            collective_id=0, has_side_effects=True, vmem_limit_bytes=48 * 2**20
+            collective_id=0, has_side_effects=True, vmem_limit_bytes=62 * 2**20
         ),
     )(probes, task_weights)
     return merged, residual

time: 67.6 us -> 65.9 us (0.975)
  local copies, waits for them, and re-layouts: 3.39 us -> 2.26 us
    unnamed x6 -> x4, local copies, waits for them, and re-layouts: 3.39 us -> 2.26 us
where the time goes in v3:
time: 65.9 us; the launch traced here: 65.7 us
  Pallas kernels  62.8 us (95%)
  local copies, waits for them, and re-layouts  2.26 us (3%)
    pallas_call x1, Pallas kernels, on_device(): pl.pallas_call(functools.partial(kernel, tasks, rows), out_shape=[jax.Sha...  62.8 us
    unnamed x4, local copies, waits for them, and re-layouts  2.26 us

profile of v3, /device:TPU:0, one launch (start us, length us, event | category | flops | bytes accessed | tf_op | source)
XLA Modules:
  0.0 65.7 jit_solution(3653913087485691689)
XLA Ops:
  0.6 62.8 %shard_map.41 = (f32[256,128]{1,0:T(8,128)}, f32[256,128]{1,0:T(8,128)}) custom-call(bf16[1,384,1024]{2,1,0:T(8,128)(2,1)} %x_hbm.1, bf16[1,1024,128]{2,1,0:T(8,128)(2,1)} %w_hbm.1), custom_call_target="tpu_custom_call" | custom-call | tf_op jit(solution)/shard_map/pallas_call | solution.py:381
  63.5 0.0 copy-start
  63.5 1.6 %copy.6 = f32[256,128]{1,0:T(8,128)} copy(f32[256,128]{1,0:T(8,128)} %get-tuple-element.4) | data formatting | bytes 262144
  65.1 0.0 copy-done
  65.1 0.7 copy.7
Async XLA Ops:
  63.5 1.6 %copy-start = (f32[256,128]{1,0:T(8,128)S(1)}, f32[256,128]{1,0:T(8,128)}, u32[]{:S(2)}) copy-start(f32[256,128]{1,0:T(8,128)} %get-tuple-element.5) | copy-start | bytes 393220
